TPU v7x, 128 devices: a whole 4x4x4 slice. The times are simulated.
128 devices in a mesh: dp: 16 (over y, z), expert: 8 (over x, core).
Axes of the slice: x: 4, y: 4, z: 4, core: 2. Of those that a mesh axis runs over, the one named last changes fastest.
Arguments:
- grad_out: bfloat16 [16384, 6144], P(('dp', 'expert')), may hold values from -6 to 6
- routes: int32 [16384, 2], P(('dp', 'expert')), may hold values from 0 to 31, all different within a row; in each aligned block of 128 rows (0 to 127, 128 to 255, ...) at most 9 rows name the same one
- loss_weight: int32 [16384], P(('dp', 'expert')), may hold values from 1 to 4
- saved_input: bfloat16 [32, 1152, 6144], P('dp', None, 'expert'), may hold values from -6 to 6
- saved_gate: bfloat16 [32, 1152, 1024], P('dp', None, 'expert'), may hold values from -8 to 8
- saved_up: bfloat16 [32, 1152, 1024], P('dp', None, 'expert'), may hold values from -6 to 6
- w_gate: bfloat16 [32, 6144, 1024], P('dp', 'expert'), may hold values from -0.1875 to 0.1875
- w_up: bfloat16 [32, 6144, 1024], P('dp', 'expert'), may hold values from -0.1875 to 0.1875
- w_down: bfloat16 [32, 1024, 6144], P('dp', None, 'expert'), may hold values from -0.078125 to 0.078125
Outputs:
- grad_input: bfloat16 [16384, 6144], P(('dp', 'expert'))
- grad_gate: bfloat16 [32, 6144, 1024], P('dp', 'expert')
- grad_up: bfloat16 [32, 6144, 1024], P('dp', 'expert')
- grad_down: bfloat16 [32, 1024, 6144], P('dp', None, 'expert')
Inputs may be any that keep to these rules, and one draw needn't show every extreme that they name: `routes`: each row names two different experts; among the rows of one device no expert is named more than 9 times, and some device names some expert exactly 9 times.
All inputs are finite; a program needn't handle non-finite values.
Results may differ from a plain program's by a relative error of at most 0.0061.
Values may be sent and summed in bfloat16 or wider, within the bound.
No kernel may reach another device: no remote copies, remote signals or barrier semaphores. Data moves between devices by JAX's collectives and lax.ppermute only.
A program may use at most 192 MiB of HBM per device.

v0:
```python
import jax
import jax.numpy as jnp
from jax import lax
from jax.sharding import PartitionSpec as P


def body(grad_out, routes, loss_weight, saved_input, saved_gate, saved_up, w_gate, w_up, w_down):
    groups = lax.axis_size("dp")
    splits = lax.axis_size("expert")
    local_experts = w_gate.shape[0]
    experts_all = local_experts * groups
    tokens_here = grad_out.shape[0]
    width = grad_out.shape[1]
    slice_width = width // splits
    slots_all = saved_input.shape[1]
    capacity = slots_all // (groups * splits)
    scaled = (
        grad_out.astype(jnp.float32) * loss_weight.astype(jnp.float32)[:, None] * 0.25
    ).astype(jnp.bfloat16)
    chosen = routes.reshape(-1)
    onehot = (chosen[:, None] == jnp.arange(experts_all, dtype=jnp.int32)[None, :]).astype(
        jnp.int32
    )
    before = jnp.cumsum(onehot, axis=0) - onehot
    rank = jnp.sum(before * onehot, axis=1)
    dest_row = (chosen % local_experts * groups + chosen // local_experts) * capacity + rank
    marks = (
        dest_row[:, None] == jnp.arange(experts_all * capacity, dtype=jnp.int32)[None, :]
    ).astype(jnp.float32)
    placed = jnp.sum(marks.reshape(tokens_here, 2, experts_all * capacity), axis=1).astype(
        jnp.bfloat16
    )
    outgoing = jnp.einsum("tr,td->rd", placed, scaled, preferred_element_type=jnp.float32).astype(
        jnp.bfloat16
    )
    ordered = outgoing.reshape(local_experts, groups, capacity, splits, slice_width)
    ordered = ordered.transpose(0, 1, 3, 2, 4).reshape(
        local_experts, groups * splits, capacity, slice_width
    )
    arrived = lax.all_to_all(ordered, ("dp", "expert"), split_axis=1, concat_axis=1, tiled=True)
    dispatched = arrived.reshape(local_experts, slots_all, slice_width)
    partial_value = jnp.einsum(
        "esd,ehd->esh", dispatched, w_down, preferred_element_type=jnp.float32
    )
    dhidden = lax.psum(partial_value, "expert")
    gates_all, ups_all = (
        lax.all_gather(saved_gate, "expert", axis=2, tiled=True),
        lax.all_gather(saved_up, "expert", axis=2, tiled=True),
    )
    gvals = gates_all.astype(jnp.float32)
    uvals = ups_all.astype(jnp.float32)
    sig = jax.nn.sigmoid(gvals)
    act = gvals * sig
    hidden = (act * uvals).astype(jnp.bfloat16)
    dgate = (dhidden * uvals * sig * (1.0 + gvals * (1.0 - sig))).astype(jnp.bfloat16)
    dup = (dhidden * act).astype(jnp.bfloat16)
    hidden, dgate, dup = (hidden, dgate, dup)
    grad_down = jnp.einsum(
        "esh,esd->ehd", hidden, dispatched, preferred_element_type=jnp.float32
    ).astype(jnp.bfloat16)
    grad_gate = jnp.einsum(
        "esd,esh->edh", saved_input, dgate, preferred_element_type=jnp.float32
    ).astype(jnp.bfloat16)
    grad_up = jnp.einsum(
        "esd,esh->edh", saved_input, dup, preferred_element_type=jnp.float32
    ).astype(jnp.bfloat16)
    slot_grad = jnp.einsum("esh,edh->esd", dgate, w_gate, preferred_element_type=jnp.float32)
    slot_grad = slot_grad + jnp.einsum(
        "esh,edh->esd", dup, w_up, preferred_element_type=jnp.float32
    )
    slot_grad = slot_grad.astype(jnp.bfloat16)
    leaving = slot_grad.reshape(local_experts, groups * splits, capacity, slice_width)
    returned = lax.all_to_all(leaving, ("dp", "expert"), split_axis=1, concat_axis=1, tiled=True)
    returned = returned.reshape(local_experts, groups, splits, capacity, slice_width).transpose(
        0, 1, 3, 2, 4
    )
    returned = returned.reshape(experts_all * capacity, width)
    grad_input = jnp.einsum(
        "tr,rd->td", placed, returned, preferred_element_type=jnp.float32
    ).astype(jnp.bfloat16)
    return (grad_input, grad_gate, grad_up, grad_down)


def solution(mesh):
    return jax.shard_map(
        body,
        mesh=mesh,
        in_specs=(
            P(("dp", "expert"), None),
            P(("dp", "expert"), None),
            P(("dp", "expert")),
            P("dp", None, "expert"),
            P("dp", None, "expert"),
            P("dp", None, "expert"),
            P("dp", "expert", None),
            P("dp", "expert", None),
            P("dp", None, "expert"),
        ),
        out_specs=(
            P(("dp", "expert"), None),
            P("dp", "expert", None),
            P("dp", "expert", None),
            P("dp", None, "expert"),
        ),
        check_vma=False,
    )
```

profile of v0, /device:TPU:1, one launch (start us, length us, event | category | flops | bytes accessed | tf_op | source)
XLA Modules:
  0.0 385.4 jit_solution(1867682180642988697)
XLA Ops:
  7.2 1.6 copy.105
  12.0 1.9 reduce-window.6
  18.2 2.6 convolution_convert_fusion
  22.3 3.6 copy.110
  25.9 57.3 %all_to_all.10 = bf16[2,128,9,768]{3,0,2,1:T(2,128)(2,1)S(1)} all-to-all(bf16[2,128,9,768]{3,0,2,1:T(2,128)(2,1)S(1)} %copy.110), channel_id=1, replica_groups=mesh['dp'=16,'expert'=8] {'dp','expert'}, dimensions={1} | all-to-all | bytes 7077888 | tf_op jit(solution)/shard_map/all_to_all | solution.py:40
  83.3 1.9 copy-done.3
  85.1 6.2 %fusion.11 = f32[2,1152,1024]{2,1,0:T(8,128)} fusion(bf16[2,1024,768]{2,1,0:T(8,128)(2,1)S(1)} %copy-done.6, bf16[2,1152,768]{2,0,1:T(2,128)(2,1)S(1)} %bitcast.56), kind=kOutput, calls=%fused_computation.23 | convolution fusion | flops 3623878656 | bytes 16121856 | tf_op jit(solution)/shard_map/esd,ehd->esh/dot_general | solution.py:42
  92.8 108.4 %all-reduce.2.cloned.1.call-done = f32[2,1152,1024]{2,1,0:T(8,128)} async-done(((f32[2,1152,1024]{2,1,0:T(8,128)}), f32[2,1152,1024]{2,1,0:T(8,128)}) %all-reduce.2.cloned.1.call-update) | async-done | bytes 9437200 | tf_op jit(solution)/shard_map/psum | solution.py:45
  201.2 40.5 %all-gather.5.cloned.1.call-done = bf16[2,1152,1024]{2,1,0:T(8,128)(2,1)} async-done(((bf16[2,1152,128]{2,1,0:T(8,128)(2,1)}), bf16[2,1152,1024]{2,1,0:T(8,128)(2,1)}) %all-gather.5.cloned.1.call-update) | async-done | bytes 4718608 | tf_op jit(solution)/shard_map/all_gather | solution.py:47
  241.8 41.0 %all-gather.3.cloned.1.call-done = bf16[2,1152,1024]{2,1,0:T(8,128)(2,1)} async-done(((bf16[2,1152,128]{2,1,0:T(8,128)(2,1)}), bf16[2,1152,1024]{2,1,0:T(8,128)(2,1)}) %all-gather.3.cloned.1.call-update) | async-done | bytes 4718608 | tf_op jit(solution)/shard_map/all_gather | solution.py:48
  282.7 9.0 %multiply_convert_fusion = (bf16[2,1152,1024]{2,1,0:T(8,128)(2,1)S(1)}, bf16[2,1152,1024]{2,1,0:T(8,128)(2,1)S(1)}) fusion(f32[2,1152,1024]{2,1,0:T(8,128)} %all-reduce.2.cloned.1.call-done, bf16[2,1152,1024]{2,1,0:T(8,128)(2,1)} %all-gather.5.cloned.1.call-done, bf16[2,1152,1024]{2,1,0:T(8,128)(2,1)} %all-gather.3.cloned.1.call-done), kind=kLoop, calls=%fused_computation.13 | loop fusion | flops 35389440 | bytes 28311552 | tf_op jit(solution)/shard_map/convert_element_type | solution.py:56
  291.8 5.9 %fusion.30 = f32[2,1152,768]{2,1,0:T(8,128)} fusion(bf16[2,1152,1024]{2,1,0:T(8,128)(2,1)S(1)} %get-tuple-element.29, bf16[2,768,1024]{2,1,0:T(8,128)(2,1)S(1)} %copy-done.7), kind=kOutput, calls=%fused_computation.51 | convolution fusion | flops 3623878656 | bytes 14942208 | tf_op jit(solution)/shard_map/esh,edh->esd/dot_general | solution.py:67
  298.2 6.1 %add_convert_fusion = bf16[2,1152,768]{2,1,0:T(8,128)(2,1)S(1)} fusion(f32[2,1152,768]{2,1,0:T(8,128)} %fusion.30, bf16[2,1152,1024]{2,1,0:T(8,128)(2,1)S(1)} %get-tuple-element.28, bf16[2,768,1024]{2,1,0:T(8,128)(2,1)S(1)} %copy-done.8), kind=kOutput, calls=%fused_computation.16 | convolution fusion | flops 3627417600 | bytes 18481152 | tf_op jit(solution)/shard_map/esh,edh->esd/dot_general | solution.py:68
  304.3 13.9 %copy.112 = bf16[2,1152,768]{2,0,1:T(2,128)(2,1)} copy(bf16[2,1152,768]{2,1,0:T(8,128)(2,1)S(1)} %add_convert_fusion) | data formatting | bytes 7077888 | tf_op jit(solution)/shard_map/convert_element_type | solution.py:71
  318.2 9.3 %all-to-all-start.1 = ((bf16[2,128,9,768]{3,0,2,1:T(2,128)(2,1)}), bf16[2,128,9,768]{3,0,2,1:T(2,128)(2,1)}, u32[]{:S(2)}, u32[]{:S(2)}) async-start(bf16[2,128,9,768]{3,0,2,1:T(2,128)(2,1)} %bitcast.52), calls=%async_computation.1 | async-start | bytes 7077888 | tf_op jit(solution)/shard_map/all_to_all | solution.py:73
  327.5 9.4 %convert_bitcast_fusion = bf16[2,768,1024]{1,2,0:T(8,128)(2,1)} fusion(bf16[2,1152,1024]{2,1,0:T(8,128)(2,1)} %copy-done.2, bf16[2,1152,768]{2,1,0:T(8,128)(2,1)S(1)} %copy-done), kind=kOutput, calls=%fused_computation.19 | convolution fusion | flops 3625451520 | bytes 11403264 | tf_op jit(solution)/shard_map/esd,esh->edh/dot_general | solution.py:64
  337.0 4.6 %copy.119 = bf16[2,768,1024]{2,1,0:T(8,128)(2,1)} copy(bf16[2,768,1024]{1,2,0:T(8,128)(2,1)} %convert_bitcast_fusion) | data formatting | bytes 6291456
  341.6 9.4 %convert_bitcast_fusion.1 = bf16[2,768,1024]{1,2,0:T(8,128)(2,1)} fusion(bf16[2,1152,1024]{2,1,0:T(8,128)(2,1)} %copy-done.1, bf16[2,1152,768]{2,1,0:T(8,128)(2,1)S(1)} %copy-done), kind=kOutput, calls=%fused_computation.20 | convolution fusion | flops 3625451520 | bytes 11403264 | tf_op jit(solution)/shard_map/esd,esh->edh/dot_general | solution.py:61
  351.0 4.6 %copy.118 = bf16[2,768,1024]{2,1,0:T(8,128)(2,1)} copy(bf16[2,768,1024]{1,2,0:T(8,128)(2,1)} %convert_bitcast_fusion.1) | data formatting | bytes 6291456
  355.6 12.1 %fusion.13 = bf16[2,1024,768]{2,1,0:T(8,128)(2,1)} fusion(bf16[2,1152,768]{2,0,1:T(2,128)(2,1)} %bitcast.57, bf16[2,1152,1024]{2,1,0:T(8,128)(2,1)} %all-gather.3.cloned.1.call-done, bf16[2,1152,1024]{2,1,0:T(8,128)(2,1)} %all-gather.5.cloned.1.call-done), kind=kOutput, calls=%fused_computation.25 | convolution fusion | flops 3644325888 | bytes 16121856 | tf_op jit(solution)/shard_map/esh,esd->ehd/dot_general | solution.py:58
  367.8 5.5 %all-to-all-done.1 = bf16[2,128,9,768]{3,0,2,1:T(2,128)(2,1)} async-done(((bf16[2,128,9,768]{3,0,2,1:T(2,128)(2,1)}), bf16[2,128,9,768]{3,0,2,1:T(2,128)(2,1)}, u32[]{:S(2)}, u32[]{:S(2)}) %all-to-all-start.1) | async-done | bytes 3538976 | tf_op jit(solution)/shard_map/all_to_all | solution.py:73
  373.2 2.5 copy.113
  375.7 1.0 copy.125
  376.7 2.2 convolution_convert_fusion.1
  (37 shorter events, 10.9 us)
Async XLA Ops:
  7.2 320.4 %copy-start = (bf16[2,1152,768]{2,1,0:T(8,128)(2,1)S(1)}, bf16[2,1152,768]{2,1,0:T(8,128)(2,1)}, u32[]{:S(2)}) copy-start(bf16[2,1152,768]{2,1,0:T(8,128)(2,1)} %param.12) | copy-start | bytes 10616836
  7.2 194.1 %all-reduce.2.cloned.1.call-start = ((), (), s32[]{:S(2)}) async-start(), calls=%async_computation.2 | async-start | bytes 18874368 | tf_op jit(solution)/shard_map/psum | solution.py:45
  18.2 2.6 copy-start.4
  25.9 59.2 %copy-start.6 = (bf16[2,1024,768]{2,1,0:T(8,128)(2,1)S(1)}, bf16[2,1024,768]{2,1,0:T(8,128)(2,1)}, u32[]{:S(2)}) copy-start(bf16[2,1024,768]{2,1,0:T(8,128)(2,1)} %param.17) | copy-start | bytes 9437188
  83.2 1.9 copy-start.3
  91.3 150.4 %all-gather.5.cloned.1.call-start = ((), (), s32[]{:S(2)}) async-start(), calls=%async_computation.4 | async-start | bytes 5308416 | tf_op jit(solution)/shard_map/all_gather | solution.py:47
  92.1 190.6 %all-gather.3.cloned.1.call-start = ((), (), s32[]{:S(2)}) async-start(), calls=%async_computation.3 | async-start | bytes 5308416 | tf_op jit(solution)/shard_map/all_gather | solution.py:48
  282.7 9.1 %copy-start.7 = (bf16[2,768,1024]{2,1,0:T(8,128)(2,1)S(1)}, bf16[2,768,1024]{2,1,0:T(8,128)(2,1)}, u32[]{:S(2)}) copy-start(bf16[2,768,1024]{2,1,0:T(8,128)(2,1)} %param.15) | copy-start | bytes 9437188
  291.8 6.0 %copy-start.1 = (bf16[2,1152,1024]{2,1,0:T(8,128)(2,1)}, bf16[2,1152,1024]{2,1,0:T(8,128)(2,1)S(1)}, u32[]{:S(2)}) copy-start(bf16[2,1152,1024]{2,1,0:T(8,128)(2,1)S(1)} %get-tuple-element.29) | copy-start | bytes 14155780
  291.8 6.4 %copy-start.2 = (bf16[2,1152,1024]{2,1,0:T(8,128)(2,1)}, bf16[2,1152,1024]{2,1,0:T(8,128)(2,1)S(1)}, u32[]{:S(2)}) copy-start(bf16[2,1152,1024]{2,1,0:T(8,128)(2,1)S(1)} %get-tuple-element.28) | copy-start | bytes 14155780
  291.8 6.4 %copy-start.8 = (bf16[2,768,1024]{2,1,0:T(8,128)(2,1)S(1)}, bf16[2,768,1024]{2,1,0:T(8,128)(2,1)}, u32[]{:S(2)}) copy-start(bf16[2,768,1024]{2,1,0:T(8,128)(2,1)} %param.16) | copy-start | bytes 9437188
  318.2 55.0 %all-to-all-start.1 = ((bf16[2,128,9,768]{3,0,2,1:T(2,128)(2,1)}), bf16[2,128,9,768]{3,0,2,1:T(2,128)(2,1)}, u32[]{:S(2)}, u32[]{:S(2)}) async-start(bf16[2,128,9,768]{3,0,2,1:T(2,128)(2,1)} %bitcast.52), calls=%async_computation.1 | async-start | bytes 7077888 | tf_op jit(solution)/shard_map/all_to_all | solution.py:73
  375.7 1.0 copy-start.5
Sparse Core Ops, SparseCore 0:
  91.5 109.7 all-reduce.1
  202.9 38.8 all-gather.4
  243.5 39.2 all-gather.2
where the time goes:
time: 386 us; the launch traced here: 385 us
  waiting for transfers between devices  197 us (51%)
  blocking collectives  57.3 us (15%)
  matrix products  54 us (14%)
  local copies, waits for them, and re-layouts  40.1 us (10%)
  other arithmetic  13.9 us (4%)
  between operations  13.9 us (4%)
  starting transfers between devices  9.56 us (2%)
    psum x1, waiting for transfers between devices, body(): dhidden = lax.psum(partial_value, 'expert')  108 us
    all_to_all x1, blocking collectives, body(): lax.all_to_all(ordered, ('dp', 'expert'), split_axis=1, concat_axis=1, ti...  57.3 us
    all_gather x1, waiting for transfers between devices, body(): lax.all_gather(saved_up, 'expert', axis=2, tiled=True)  41 us
    all_gather x1, waiting for transfers between devices, body(): lax.all_gather(saved_gate, 'expert', axis=2, tiled=True)  40.5 us
    unnamed x23, local copies, waits for them, and re-layouts  15.2 us
    convert_element_type x1, local copies, waits for them, and re-layouts, body(): slot_grad = slot_grad.astype(jnp.bfloat16)  13.9 us
    dot_general x1, matrix products, body(): jnp.einsum('esh,esd->ehd', hidden, dispatched, preferred_element_type=jnp...  12.1 us
    dot_general x1, matrix products, body(): jnp.einsum('esd,esh->edh', saved_input, dup, preferred_element_type=jnp.f...  9.43 us
  transfers between devices with their start and end apart: 4, of which 4 were waited for; matrix products, arithmetic and copies ran while one was open for 10% of the time, Pallas kernels for 0%

commit v1 on v0

--- a/solution.py
+++ b/solution.py
@@ -42,7 +42,9 @@
     partial_value = jnp.einsum(
         "esd,ehd->esh", dispatched, w_down, preferred_element_type=jnp.float32
     )
-    dhidden = lax.psum(partial_value, "expert")
+    dhidden = partial_value
+    for hop in (1, 2, 4):
+        dhidden = dhidden + lax.ppermute(dhidden, "expert", [(dev, dev ^ hop) for dev in range(8)])
     gates_all, ups_all = (
         lax.all_gather(saved_gate, "expert", axis=2, tiled=True),
         lax.all_gather(saved_up, "expert", axis=2, tiled=True),

time: 386 us -> 692 us (1.79); the launches traced: 385 us -> 684 us
  waiting for transfers between devices: 197 us -> 466 us
  other arithmetic: 13.9 us -> 42.6 us
    ppermute x0 -> x3, waiting for transfers between devices: none -> 402 us  [body(): lax.ppermute(dhidden, 'expert', [(dev, dev ^ hop) for dev in range(8)])]
    psum x1 -> x0, waiting for transfers between devices: 108 us -> none  [body(): dhidden = lax.psum(partial_value, 'expert')]
    all_gather x1, waiting for transfers between devices: 40.5 us -> 0.02 us  [body(): lax.all_gather(saved_gate, 'expert', axis=2, tiled=True)]
    add x0 -> x2, other arithmetic: none -> 26.8 us  [body(): dhidden + lax.ppermute(dhidden, 'expert', [(dev, dev ^ hop) for dev in ra...]
    all_gather x1, waiting for transfers between devices: 41 us -> 58.6 us  [body(): lax.all_gather(saved_up, 'expert', axis=2, tiled=True)]
    unnamed x23 -> x25, local copies, waits for them, and re-layouts: 15.2 us -> 17.1 us
  transfers between devices with their start and end apart: 4 -> 6, of which waited for: 4 -> 5; matrix products, arithmetic and copies ran while one was open for 10% -> 8% of each run, Pallas kernels for 0% -> 0%
where the time goes in v1:
time: 692 us; the launch traced here: 684 us
  waiting for transfers between devices  466 us (67%)
  blocking collectives  57.3 us (8%)
  matrix products  51.8 us (7%)
  other arithmetic  42.6 us (6%)
  local copies, waits for them, and re-layouts  42.1 us (6%)
  between operations  14.5 us (2%)
  starting transfers between devices  9.14 us (1%)
    ppermute x3, waiting for transfers between devices, body(): lax.ppermute(dhidden, 'expert', [(dev, dev ^ hop) for dev in range(8)])  402 us
    all_gather x1, waiting for transfers between devices, body(): lax.all_gather(saved_up, 'expert', axis=2, tiled=True)  58.6 us
    all_to_all x1, blocking collectives, body(): lax.all_to_all(ordered, ('dp', 'expert'), split_axis=1, concat_axis=1, ti...  57.3 us
    add x2, other arithmetic, body(): dhidden + lax.ppermute(dhidden, 'expert', [(dev, dev ^ hop) for dev in ra...  26.8 us
    unnamed x25, local copies, waits for them, and re-layouts  17.1 us
    convert_element_type x1, local copies, waits for them, and re-layouts, body(): slot_grad = slot_grad.astype(jnp.bfloat16)  13.9 us
  transfers between devices with their start and end apart: 6, of which 5 were waited for; matrix products, arithmetic and copies ran while one was open for 8% of the time, Pallas kernels for 0%

profile of v1, /device:TPU:1, one launch (start us, length us, event | category | flops | bytes accessed | tf_op | source)
XLA Modules:
  0.0 683.6 jit_solution(5449744582614640258)
XLA Ops:
  18.2 2.6 convolution_convert_fusion
  22.3 3.6 copy.110
  25.9 57.3 %all_to_all.10 = bf16[2,128,9,768]{3,0,2,1:T(2,128)(2,1)S(1)} all-to-all(bf16[2,128,9,768]{3,0,2,1:T(2,128)(2,1)S(1)} %copy.110), channel_id=1, replica_groups=mesh['dp'=16,'expert'=8] {'dp','expert'}, dimensions={1} | all-to-all | bytes 7077888 | tf_op jit(solution)/shard_map/all_to_all | solution.py:40
  83.3 3.9 fusion.11
  87.2 3.6 copy-done.1
  92.1 14.4 %collective-permute-done = f32[2,1152,1024]{2,1,0:T(8,128)} collective-permute-done((f32[2,1152,1024]{2,1,0:T(8,128)S(1)}, f32[2,1152,1024]{2,1,0:T(8,128)}, u32[]{:S(2)}, u32[]{:S(2)}) %collective-permute-start) | collective-permute-done | bytes 9437216 | tf_op jit(solution)/shard_map/ppermute | solution.py:47
  106.5 13.4 %add.50 = f32[2,1152,1024]{2,1,0:T(8,128)} add(f32[2,1152,1024]{2,1,0:T(8,128)} %copy-done.1, f32[2,1152,1024]{2,1,0:T(8,128)} %collective-permute-done) | non-fusion elementwise | flops 2359296 | bytes 28311552 | tf_op jit(solution)/shard_map/add | solution.py:47
  120.3 223.0 %collective-permute-done.1 = f32[2,1152,1024]{2,1,0:T(8,128)} collective-permute-done((f32[2,1152,1024]{2,1,0:T(8,128)}, f32[2,1152,1024]{2,1,0:T(8,128)}, u32[]{:S(2)}, u32[]{:S(2)}) %collective-permute-start.1) | collective-permute-done | bytes 9437216 | tf_op jit(solution)/shard_map/ppermute | solution.py:47
  343.3 13.4 %add.51 = f32[2,1152,1024]{2,1,0:T(8,128)} add(f32[2,1152,1024]{2,1,0:T(8,128)} %add.50, f32[2,1152,1024]{2,1,0:T(8,128)} %collective-permute-done.1) | non-fusion elementwise | flops 2359296 | bytes 28311552 | tf_op jit(solution)/shard_map/add | solution.py:47
  357.3 58.6 %all-gather.3.cloned.1.call-done = bf16[2,1152,1024]{2,1,0:T(8,128)(2,1)} async-done(((bf16[2,1152,128]{2,1,0:T(8,128)(2,1)}), bf16[2,1152,1024]{2,1,0:T(8,128)(2,1)}) %all-gather.3.cloned.1.call-update) | async-done | bytes 4718608 | tf_op jit(solution)/shard_map/all_gather | solution.py:50
  415.9 164.8 %collective-permute-done.2 = f32[2,1152,1024]{2,1,0:T(8,128)} collective-permute-done((f32[2,1152,1024]{2,1,0:T(8,128)}, f32[2,1152,1024]{2,1,0:T(8,128)}, u32[]{:S(2)}, u32[]{:S(2)}) %collective-permute-start.2) | collective-permute-done | bytes 9437216 | tf_op jit(solution)/shard_map/ppermute | solution.py:47
  580.7 11.0 %multiply_convert_fusion = (bf16[2,1152,1024]{2,1,0:T(8,128)(2,1)S(1)}, bf16[2,1152,1024]{2,1,0:T(8,128)(2,1)S(1)}) fusion(f32[2,1152,1024]{2,1,0:T(8,128)} %add.51, f32[2,1152,1024]{2,1,0:T(8,128)} %collective-permute-done.2, bf16[2,1152,1024]{2,1,0:T(8,128)(2,1)} %all-gather.5.cloned.1.call-done, bf16[2,1152,1024]{2,1,0:T(8,128)(2,1)} %all-gather.3.cloned.1.call-done), kind=kLoop, calls=%fused_computation.13 | loop fusion | flops 37748736 | bytes 37748736 | tf_op jit(solution)/shard_map/convert_element_type | solution.py:58
  591.8 5.9 fusion.30
  598.1 6.1 add_convert_fusion
  604.3 13.9 %copy.112 = bf16[2,1152,768]{2,0,1:T(2,128)(2,1)} copy(bf16[2,1152,768]{2,1,0:T(8,128)(2,1)S(1)} %add_convert_fusion) | data formatting | bytes 7077888 | tf_op jit(solution)/shard_map/convert_element_type | solution.py:73
  618.2 6.9 %all-to-all-start.1 = ((bf16[2,128,9,768]{3,0,2,1:T(2,128)(2,1)}), bf16[2,128,9,768]{3,0,2,1:T(2,128)(2,1)}, u32[]{:S(2)}, u32[]{:S(2)}) async-start(bf16[2,128,9,768]{3,0,2,1:T(2,128)(2,1)} %bitcast.52), calls=%async_computation.1 | async-start | bytes 7077888 | tf_op jit(solution)/shard_map/all_to_all | solution.py:75
  625.1 12.2 %fusion.13 = bf16[2,1024,768]{2,1,0:T(8,128)(2,1)} fusion(bf16[2,1152,768]{2,0,1:T(2,128)(2,1)} %bitcast.57, bf16[2,1152,1024]{2,1,0:T(8,128)(2,1)} %all-gather.3.cloned.1.call-done, bf16[2,1152,1024]{2,1,0:T(8,128)(2,1)} %all-gather.5.cloned.1.call-done), kind=kOutput, calls=%fused_computation.25 | convolution fusion | flops 3644325888 | bytes 16121856 | tf_op jit(solution)/shard_map/esh,esd->ehd/dot_general | solution.py:60
  637.3 9.4 %convert_bitcast_fusion = bf16[2,768,1024]{1,2,0:T(8,128)(2,1)} fusion(bf16[2,1152,1024]{2,1,0:T(8,128)(2,1)} %copy-done.3, bf16[2,1152,768]{2,1,0:T(8,128)(2,1)S(1)} %copy-done), kind=kOutput, calls=%fused_computation.19 | convolution fusion | flops 3625451520 | bytes 11403264 | tf_op jit(solution)/shard_map/esd,esh->edh/dot_general | solution.py:66
  646.7 4.6 copy.119
  651.4 9.5 %convert_bitcast_fusion.1 = bf16[2,768,1024]{1,2,0:T(8,128)(2,1)} fusion(bf16[2,1152,1024]{2,1,0:T(8,128)(2,1)} %copy-done.2, bf16[2,1152,768]{2,1,0:T(8,128)(2,1)S(1)} %copy-done), kind=kOutput, calls=%fused_computation.20 | convolution fusion | flops 3625451520 | bytes 11403264 | tf_op jit(solution)/shard_map/esd,esh->edh/dot_general | solution.py:63
  660.9 4.8 copy.118
  665.7 5.1 all-to-all-done.1
  670.9 2.5 copy.113
  674.4 2.2 convolution_convert_fusion.1
  (44 shorter events, 16.1 us)
Async XLA Ops:
  7.2 630.1 %copy-start = (bf16[2,1152,768]{2,1,0:T(8,128)(2,1)S(1)}, bf16[2,1152,768]{2,1,0:T(8,128)(2,1)}, u32[]{:S(2)}) copy-start(bf16[2,1152,768]{2,1,0:T(8,128)(2,1)} %param.12) | copy-start | bytes 10616836
  7.2 350.1 %all-gather.5.cloned.1.call-start = ((), (), s32[]{:S(2)}) async-start(), calls=%async_computation.3 | async-start | bytes 5308416 | tf_op jit(solution)/shard_map/all_gather | solution.py:49
  18.2 2.6 copy-start.5
  25.9 57.3 %copy-start.7 = (bf16[2,1024,768]{2,1,0:T(8,128)(2,1)S(1)}, bf16[2,1024,768]{2,1,0:T(8,128)(2,1)}, u32[]{:S(2)}) copy-start(bf16[2,1024,768]{2,1,0:T(8,128)(2,1)} %param.17) | copy-start | bytes 9437188
  83.3 3.9 copy-start.4
  87.1 3.7 copy-start.1
  90.8 15.7 %collective-permute-start = (f32[2,1152,1024]{2,1,0:T(8,128)S(1)}, f32[2,1152,1024]{2,1,0:T(8,128)}, u32[]{:S(2)}, u32[]{:S(2)}) collective-permute-start(f32[2,1152,1024]{2,1,0:T(8,128)S(1)} %fusion.11), channel_id=1, source_target_pairs={{0,1},{1,0},{2,3},{3,2},{4,5},{5,4},{6,7},{7,6},{8,9},{9,8},{10,11... | collective-permute-start | bytes 28311560 | tf_op jit(solution)/shard_map/ppermute | solution.py:47
  119.9 223.4 %collective-permute-start.1 = (f32[2,1152,1024]{2,1,0:T(8,128)}, f32[2,1152,1024]{2,1,0:T(8,128)}, u32[]{:S(2)}, u32[]{:S(2)}) collective-permute-start(f32[2,1152,1024]{2,1,0:T(8,128)} %add.50), channel_id=1, source_target_pairs={{0,2},{1,3},{2,0},{3,1},{4,6},{5,7},{6,4},{7,5},{8,10},{9,11},{10,... | collective-permute-start | bytes 28311560 | tf_op jit(solution)/shard_map/ppermute | solution.py:47
  120.2 295.7 %all-gather.3.cloned.1.call-start = ((), (), s32[]{:S(2)}) async-start(), calls=%async_computation.2 | async-start | bytes 5308416 | tf_op jit(solution)/shard_map/all_gather | solution.py:50
  356.7 224.0 %collective-permute-start.2 = (f32[2,1152,1024]{2,1,0:T(8,128)}, f32[2,1152,1024]{2,1,0:T(8,128)}, u32[]{:S(2)}, u32[]{:S(2)}) collective-permute-start(f32[2,1152,1024]{2,1,0:T(8,128)} %add.51), channel_id=1, source_target_pairs={{0,4},{1,5},{2,6},{3,7},{4,0},{5,1},{6,2},{7,3},{8,12},{9,13},{10,... | collective-permute-start | bytes 28311560 | tf_op jit(solution)/shard_map/ppermute | solution.py:47
  415.9 175.9 %copy-start.8 = (bf16[2,768,1024]{2,1,0:T(8,128)(2,1)S(1)}, bf16[2,768,1024]{2,1,0:T(8,128)(2,1)}, u32[]{:S(2)}) copy-start(bf16[2,768,1024]{2,1,0:T(8,128)(2,1)} %param.16) | copy-start | bytes 9437188
  591.7 6.0 copy-start.3
  591.8 6.4 copy-start.2
  591.8 6.4 copy-start.9
  618.2 52.7 %all-to-all-start.1 = ((bf16[2,128,9,768]{3,0,2,1:T(2,128)(2,1)}), bf16[2,128,9,768]{3,0,2,1:T(2,128)(2,1)}, u32[]{:S(2)}, u32[]{:S(2)}) async-start(bf16[2,128,9,768]{3,0,2,1:T(2,128)(2,1)} %bitcast.52), calls=%async_computation.1 | async-start | bytes 7077888 | tf_op jit(solution)/shard_map/all_to_all | solution.py:75
  673.3 1.0 copy-start.6
Sparse Core Ops, SparseCore 0:
  120.3 51.0 all-gather.4
  357.3 58.5 all-gather.2
